TPU v7x, 768 devices: a whole 4x8x12 slice. The times are simulated.
768 devices in a mesh: dp: 8 (over x, core), row: 12 (over z), col: 8 (over y).
Axes of the slice: x: 4, y: 8, z: 12, core: 2. Of those that a mesh axis runs over, the one named last changes fastest.
Arguments:
- inputs: bfloat16 [2048, 9216], P('dp', 'row'), may hold values from -24 to 24
- out_grad: bfloat16 [2048, 49152], P('dp', 'col'), may hold values from -0.22097087 to 0.22097087
- weight: bfloat16 [49152, 9216], P(('col', 'dp'), 'row'), may hold values from -3 to 3
- ff_old: float32 [49152], P(('col', 'dp')), may hold values from 0.1 to 4
- d_old: float32 [9216], P('row'), may hold values from 0.05 to 0.5
Outputs:
- update: bfloat16 [49152, 9216], P(('col', 'dp'), 'row')
- new_weight: bfloat16 [49152, 9216], P(('col', 'dp'), 'row')
- ff_new: float32 [49152], P(('col', 'dp'))
- d_new: float32 [9216], P('row')
All inputs are finite; a program needn't handle non-finite values.
Results may differ from a plain program's by a relative error of at most 0.018.
Values may be sent and summed in bfloat16 or wider, within the bound.
A program may use at most 64 MiB of HBM per device.

v0:
```python
import jax
import jax.numpy as jnp
from jax import lax
from jax.sharding import PartitionSpec as P

D = 9216
FF = 49152


DECAY_RATE = 1.0 - 10.0 ** (-0.8)
SQUARE_EPS = 1e-30
LEARNING_RATE = 0.02


def body(inputs, out_grad, weight, ff_old, d_old):
    entries = float(FF * D)
    master = weight.astype(jnp.float32)
    gradient = lax.psum_scatter(
        lax.dot_general(
            out_grad, inputs, (((0,), (0,)), ((), ())), preferred_element_type=jnp.float32
        ).astype(jnp.bfloat16),
        "dp",
        scatter_dimension=0,
        tiled=True,
    ).astype(jnp.float32)
    squares = gradient * gradient + SQUARE_EPS
    ff_local = jnp.sum(squares, axis=1)
    d_local = jnp.sum(squares, axis=0)
    ff_total = lax.psum(ff_local, "row")
    ff_new = DECAY_RATE * ff_old + (1.0 - DECAY_RATE) * ff_total / D
    d_total, ff_sum = lax.psum((d_local, jnp.sum(ff_new)), ("dp", "col"))
    ff_mean = ff_sum / FF
    d_new = DECAY_RATE * d_old + (1.0 - DECAY_RATE) * d_total / FF
    scaled = gradient / jnp.sqrt(ff_new[:, None] * d_new[None, :] / ff_mean)
    scaled_total = lax.psum(jnp.sum(scaled * scaled), ("dp", "row", "col"))
    clip_factor = jnp.maximum(1.0, jnp.sqrt(scaled_total / entries))
    clipped = scaled / clip_factor
    return (
        clipped.astype(jnp.bfloat16),
        (master - LEARNING_RATE * clipped).astype(jnp.bfloat16),
        ff_new,
        d_new,
    )


def solution(mesh):
    return jax.shard_map(
        body,
        mesh=mesh,
        in_specs=(
            P("dp", "row"),
            P("dp", "col"),
            P(("col", "dp"), "row"),
            P(("col", "dp")),
            P("row"),
        ),
        out_specs=(P(("col", "dp"), "row"), P(("col", "dp"), "row"), P(("col", "dp")), P("row")),
        check_vma=False,
    )
```

profile of v0, /device:TPU:1, one launch (start us, length us, event | category | flops | bytes accessed | tf_op | source)
XLA Modules:
  0.0 363.0 jit_solution(10093822496823943498)
XLA Ops:
  7.2 0.0 copy-start
  7.2 0.0 reduce-scatter.2.cloned.1.call-start
  7.2 1.8 copy-done
  9.1 6.1 %convolution_convert_fusion = bf16[6144,768]{1,0:T(8,128)(2,1)} fusion(bf16[256,6144]{1,0:T(8,128)(2,1)S(1)} %copy-done, bf16[256,768]{1,0:T(8,128)(2,1)} %param.5), kind=kOutput, calls=%fused_computation | convolution fusion | flops 2420637696 | bytes 12976128 | tf_op jit(solution)/shard_map/dot_general | solution.py:19
  15.1 0.0 copy-start.3
  15.1 0.0 copy-start.4
  15.1 0.0 reduce-scatter.2.cloned.1.call-update
  15.2 72.7 %reduce-scatter.2.cloned.1.call-done = bf16[768,768]{1,0:T(8,128)(2,1)} async-done(((bf16[6144,768]{1,0:T(8,128)(2,1)}), bf16[768,768]{1,0:T(8,128)(2,1)}) %reduce-scatter.2.cloned.1.call-update) | async-done | bytes 1179664 | tf_op jit(solution)/shard_map/reduce_scatter | solution.py:18
  87.8 1.8 fusion.1
  89.6 20.0 %psum.28 = f32[768]{0:T(1024)S(1)} all-reduce(f32[768]{0:T(1024)S(1)} %get-tuple-element.5), channel_id=1, replica_groups=mesh['dp'=8,'row'=12,'col'=8] {'row'}, use_global_device_ids=true, to_apply=%region_2.0 | all-reduce | flops 768 | bytes 6144 | tf_op jit(solution)/shard_map/psum | solution.py:29
  109.6 0.0 copy-done.3
  109.6 0.6 fusion.4
  110.2 0.0 copy-start.1
  110.2 125.8 %all-reduce = (f32[]{:T(128)}, f32[768]{0:T(1024)S(1)}) all-reduce(f32[]{:T(128)} %get-tuple-element.8, f32[768]{0:T(1024)S(1)} %get-tuple-element.4), channel_id=1, replica_groups=mesh['dp'=8,'row'=12,'col'=8] {'dp','col'}, use_global_device_ids=true, to_apply=%region_6.0 | all-reduce | flops 769 | bytes 6152 | tf_op jit(solution)/shard_map/psum | solution.py:31
  236.6 0.0 copy-done.4
  236.7 0.0 copy-start.2
  236.7 2.9 multiply_reduce_fusion
  239.6 112.0 %psum.31 = f32[]{:T(128)} all-reduce(f32[]{:T(128)} %multiply_reduce_fusion), channel_id=1, replica_groups=mesh['dp'=8,'row'=12,'col'=8] {'dp','row','col'}, use_global_device_ids=true, to_apply=%region_8.0 | all-reduce | flops 1 | bytes 8 | tf_op jit(solution)/shard_map/psum | solution.py:35
  352.3 3.9 %subtract_convert_fusion = (bf16[768,768]{1,0:T(8,128)(2,1)}, bf16[768,768]{1,0:T(8,128)(2,1)}) fusion(bf16[768,768]{1,0:T(8,128)(2,1)} %param.7, f32[]{:T(128)S(6)} %max_shard_map.3, f32[]{:T(128)S(6)} %div.37, f32[768]{0:T(1024)S(1)} %multiply_add_fusion, f32[768]{0:T(1024)S(1)} %get-tuple-element.9, bf16[768,768]{1,0:T(8,128)(2,1)} %reduce-scatter.2.cloned.1.call-done), kind=kLoop, calls=%fused_computation.6 | loop fusion | flops 5898240 | bytes 4724744 | tf_op jit(solution)/shard_map/convert_element_type | solution.py:40
  356.1 0.0 copy-done.1
  356.1 0.0 copy-done.2
  (1 shorter events, 0.0 us)
Async XLA Ops:
  7.2 1.9 copy-start
  7.2 80.6 %reduce-scatter.2.cloned.1.call-start = ((), (), s32[]{:S(2)}) async-start(), calls=%async_computation.1 | async-start | bytes 10616832 | tf_op jit(solution)/shard_map/reduce_scatter | solution.py:18
  15.1 94.5 %copy-start.3 = (f32[768]{0:T(1024)S(1)}, f32[768]{0:T(1024)}, u32[]{:S(2)}) copy-start(f32[768]{0:T(1024)} %param.8) | copy-start | bytes 9220
  15.1 221.5 %copy-start.4 = (f32[768]{0:T(1024)S(1)}, f32[768]{0:T(1024)}, u32[]{:S(2)}) copy-start(f32[768]{0:T(1024)} %param.9) | copy-start | bytes 9220
  110.2 245.9 %copy-start.1 = (f32[768]{0:T(1024)}, f32[768]{0:T(1024)S(1)}, u32[]{:S(2)}) copy-start(f32[768]{0:T(1024)S(1)} %get-tuple-element.9) | copy-start | bytes 9220
  236.7 119.5 %copy-start.2 = (f32[768]{0:T(1024)}, f32[768]{0:T(1024)S(1)}, u32[]{:S(2)}) copy-start(f32[768]{0:T(1024)S(1)} %multiply_add_fusion) | copy-start | bytes 9220
Sparse Core Ops, SparseCore 0:
  15.3 72.4 reduce-scatter.1
where the time goes:
time: 363 us
  blocking collectives  258 us (71%)
  waiting for transfers between devices  72.7 us (20%)
  between operations  15.4 us (4%)
  other arithmetic  9.17 us (3%)
  matrix products  6.08 us (2%)
    psum x1, blocking collectives, body(): d_total, ff_sum = lax.psum((d_local, jnp.sum(ff_new)), ('dp', 'col'))  126 us
    psum x1, blocking collectives, body(): scaled_total = lax.psum(jnp.sum(scaled * scaled), ('dp', 'row', 'col'))  112 us
    reduce_scatter x1, waiting for transfers between devices, body(): lax.psum_scatter(lax.dot_general(out_grad, inputs, (((0,), (0,)), ((), ()...  72.7 us
    psum x1, blocking collectives, body(): ff_total = lax.psum(ff_local, 'row')  20 us
  transfers between devices with their start and end apart: 1, of which 1 were waited for; matrix products, arithmetic and copies ran while one was open for 0% of the time, Pallas kernels for 0%

commit v1 on v0

v1 whole, which is shorter than its diff:
```python
import functools

import jax
import jax.numpy as jnp
from jax import lax
from jax.experimental import pallas as pl
from jax.experimental.pallas import tpu as pltpu
from jax.sharding import PartitionSpec as P

D = 9216
FF = 49152

DECAY_RATE = 1.0 - 10.0 ** (-0.8)
SQUARE_EPS = 1e-30
LEARNING_RATE = 0.02

MESH = pl.DeviceIdType.MESH
LANES = 128


def kernel(sizes, d_full, ff_full, inp, og, w_hbm, ff_old, d_old, upd_ref, new_ref, ff_ref, d_ref,
           a_buf, b_buf, w_buf, g, row_t, ff_buf, xy_buf, col_buf, t_buf,
           a_send, a_recv, b_send, b_recv, loc, s_send, ff_recv, xy_recv, col_recv, t_recv):
    n_dp, n_row, n_col = sizes
    dp, row, col = (lax.axis_index(a) for a in ("dp", "row", "col"))
    tok, width = inp.shape
    units = g.shape[0]
    blocks = units // LANES
    lane_blocks = width // LANES

    barrier = pltpu.get_barrier_semaphore()
    for axis, n, me in (("dp", n_dp, dp), ("row", n_row, row), ("col", n_col, col)):
        def greet(i, _, axis=axis, n=n, me=me):
            pl.semaphore_signal(barrier, inc=1, device_id={axis: lax.rem(me + i, n)}, device_id_type=MESH)
            return 0
        lax.fori_loop(1, n, greet, 0)

    def unit_cols(i):
        return pl.ds(pl.multiple_of(i * units, LANES), units)

    own_a = pltpu.make_async_copy(og.at[:, unit_cols(dp)], a_buf.at[dp], loc.at[0])
    own_b = pltpu.make_async_copy(inp, b_buf.at[dp], loc.at[1])
    own_w = pltpu.make_async_copy(w_hbm, w_buf, loc.at[2])
    own_a.start()
    own_b.start()
    own_w.start()
    pl.semaphore_wait(barrier, n_dp + n_row + n_col - 3)

    def send_a(i):
        to = lax.rem(dp + i, n_dp)
        return pltpu.make_async_remote_copy(og.at[:, unit_cols(to)], a_buf.at[dp], a_send.at[i], a_recv.at[dp],
                                            device_id={"dp": to}, device_id_type=MESH)

    def send_b(i):
        to = lax.rem(dp + i, n_dp)
        return pltpu.make_async_remote_copy(inp, b_buf.at[dp], b_send.at[i], b_recv.at[dp],
                                            device_id={"dp": to}, device_id_type=MESH)

    def start_sends(i, _):
        send_a(i).start()
        send_b(i).start()
        return 0
    lax.fori_loop(1, n_dp, start_sends, 0)

    def product(src):
        return lax.dot_general(a_buf[src], b_buf[src], (((0,), (0,)), ((), ())), preferred_element_type=jnp.float32)

    own_a.wait()
    own_b.wait()
    g[...] = product(dp)

    def take(i, _):
        src = lax.rem(dp + n_dp - i, n_dp)
        pltpu.make_async_remote_copy(a_buf.at[src], a_buf.at[src], a_send.at[0], a_recv.at[src],
                                     device_id={"dp": src}, device_id_type=MESH).wait_recv()
        pltpu.make_async_remote_copy(b_buf.at[src], b_buf.at[src], b_send.at[0], b_recv.at[src],
                                     device_id={"dp": src}, device_id_type=MESH).wait_recv()
        g[...] += product(src)
        return 0
    lax.fori_loop(1, n_dp, take, 0)

    def exchange(axis, n, me, buf, recv):
        def copy(i):
            to = lax.rem(me + i, n)
            return pltpu.make_async_remote_copy(buf.at[me], buf.at[me], s_send.at[i], recv.at[me],
                                                device_id={axis: to}, device_id_type=MESH)

        def start(i, _):
            copy(i).start()
            return 0
        lax.fori_loop(1, n, start, 0)

        def arrive(i, _):
            src = lax.rem(me + n - i, n)
            pltpu.make_async_remote_copy(buf.at[src], buf.at[src], s_send.at[0], recv.at[src],
                                         device_id={axis: src}, device_id_type=MESH).wait_recv()
            return 0
        lax.fori_loop(1, n, arrive, 0)

        def sent(i, _):
            copy(i).wait_send()
            return 0
        lax.fori_loop(1, n, sent, 0)
        total = buf[0]
        for i in range(1, n):
            total = total + buf[i]
        return total

    ff_buf[row] = jnp.zeros(ff_buf.shape[1:], jnp.float32)
    xy_buf[dp] = jnp.zeros(xy_buf.shape[1:], jnp.float32)
    d_part = [jnp.zeros((1, LANES), jnp.float32)] * lane_blocks
    for k in range(blocks):
        rows = pl.ds(k * LANES, LANES)
        part = None
        for j in range(lane_blocks):
            v = g[rows, pl.ds(j * LANES, LANES)]
            sq = v * v + SQUARE_EPS
            part = sq if part is None else part + sq
            d_part[j] = d_part[j] + jnp.sum(sq, axis=0, keepdims=True)
        ff_buf[row, pl.ds(k, 1), :] = jnp.sum(part.T, axis=0, keepdims=True)
    for j in range(lane_blocks):
        xy_buf[dp, pl.ds(j, 1), :] = d_part[j]

    ff_total = exchange("row", n_row, row, ff_buf, ff_recv)[:blocks]
    ff_new = DECAY_RATE * ff_old[...] + (1.0 - DECAY_RATE) * ff_total / d_full
    ff_ref[...] = ff_new
    inv = 1.0 / ff_new

    q_part = [jnp.zeros((1, LANES), jnp.float32)] * lane_blocks
    for k in range(blocks):
        rows = pl.ds(k * LANES, LANES)
        u = jnp.broadcast_to(inv[k:k + 1], (LANES, LANES)).T
        for j in range(lane_blocks):
            v = g[rows, pl.ds(j * LANES, LANES)]
            q_part[j] = q_part[j] + jnp.sum(v * v * u, axis=0, keepdims=True)
    for j in range(lane_blocks):
        xy_buf[dp, pl.ds(lane_blocks + j, 1), :] = q_part[j]
    xy_buf[dp, pl.ds(2 * lane_blocks, 1), :] = jnp.sum(ff_new, axis=0, keepdims=True)

    col_buf[col] = exchange("dp", n_dp, dp, xy_buf, xy_recv)
    total = exchange("col", n_col, col, col_buf, col_recv)
    d_new = DECAY_RATE * d_old[...] + (1.0 - DECAY_RATE) * total[:lane_blocks] / ff_full
    d_ref[...] = d_new
    ff_mean = jnp.sum(total[2 * lane_blocks:2 * lane_blocks + 1], axis=1, keepdims=True) / ff_full
    t_buf[row] = jnp.zeros(t_buf.shape[1:], jnp.float32)
    t_buf[row, pl.ds(0, lane_blocks), :] = total[lane_blocks:2 * lane_blocks] / d_new
    t_total = exchange("row", n_row, row, t_buf, t_recv)
    square_mean = jnp.sum(jnp.sum(t_total, axis=0, keepdims=True), axis=1, keepdims=True) * ff_mean / (d_full * ff_full)
    factor = jnp.sqrt(ff_mean) / jnp.maximum(1.0, jnp.sqrt(square_mean))
    own_w.wait()
    inv_d = lax.rsqrt(d_new) * factor
    inv_f = lax.rsqrt(ff_new)
    for k in range(blocks):
        rows = pl.ds(k * LANES, LANES)
        u = jnp.broadcast_to(inv_f[k:k + 1], (LANES, LANES)).T
        for j in range(lane_blocks):
            cols = pl.ds(j * LANES, LANES)
            clipped = g[rows, cols] * u * inv_d[j:j + 1]
            upd_ref[rows, cols] = clipped.astype(jnp.bfloat16)
            new_ref[rows, cols] = (w_buf[rows, cols].astype(jnp.float32) - LEARNING_RATE * clipped).astype(jnp.bfloat16)

    def drain(i, _):
        send_a(i).wait_send()
        send_b(i).wait_send()
        return 0
    lax.fori_loop(1, n_dp, drain, 0)


def solution(mesh):
    sizes = n_dp, n_row, n_col = tuple(mesh.shape[a] for a in ("dp", "row", "col"))

    def body(inputs, out_grad, weight, ff_old, d_old):
        tok, width = inputs.shape
        units = weight.shape[0]
        hbm = pl.BlockSpec(memory_space=pl.ANY)
        vmem = pl.BlockSpec(memory_space=pltpu.VMEM)
        f32, bf16 = jnp.float32, jnp.bfloat16
        fr, dr = units // LANES, width // LANES
        dma = pltpu.SemaphoreType.DMA
        upd, new, ff_new, d_new = pl.pallas_call(
            functools.partial(kernel, sizes, float(width * n_row), float(units * n_dp * n_col)),
            out_shape=(
                jax.ShapeDtypeStruct((units, width), bf16),
                jax.ShapeDtypeStruct((units, width), bf16),
                jax.ShapeDtypeStruct((fr, LANES), f32),
                jax.ShapeDtypeStruct((dr, LANES), f32),
            ),
            in_specs=[hbm, hbm, hbm, vmem, vmem],
            out_specs=(vmem, vmem, vmem, vmem),
            scratch_shapes=[
                pltpu.VMEM((n_dp, tok, units), bf16),
                pltpu.VMEM((n_dp, tok, width), bf16),
                pltpu.VMEM((units, width), bf16),
                pltpu.VMEM((units, width), f32),
                pltpu.VMEM((units, LANES), f32),
                pltpu.VMEM((n_row, 8, LANES), f32),
                pltpu.VMEM((n_dp, 16, LANES), f32),
                pltpu.VMEM((n_col, 16, LANES), f32),
                pltpu.VMEM((n_row, 8, LANES), f32),
                dma((n_dp,)), dma((n_dp,)), dma((n_dp,)), dma((n_dp,)), dma((3,)),
                dma((max(sizes),)), dma((n_row,)), dma((n_dp,)), dma((n_col,)), dma((n_row,)),
            ],
            compiler_params=pltpu.CompilerParams(collective_id=0, has_side_effects=True, vmem_limit_bytes=50 * 2**20),
        )(inputs, out_grad, weight, ff_old.reshape(fr, LANES), d_old.reshape(dr, LANES))
        return upd, new, ff_new.reshape(units), d_new.reshape(width)

    return jax.shard_map(
        body,
        mesh=mesh,
        in_specs=(
            P("dp", "row"),
            P("dp", "col"),
            P(("col", "dp"), "row"),
            P(("col", "dp")),
            P("row"),
        ),
        out_specs=(P(("col", "dp"), "row"), P(("col", "dp"), "row"), P(("col", "dp")), P("row")),
        check_vma=False,
    )
```

time: 363 us -> 119 us (0.33)
  blocking collectives: 258 us -> 0 us
  Pallas kernels: 0 us -> 110 us
  waiting for transfers between devices: 72.7 us -> 0 us
  between operations: 15.4 us -> 0.65 us
  other arithmetic: 9.17 us -> 0 us
  matrix products: 6.08 us -> 0 us
  local copies, waits for them, and re-layouts: 1.86 us -> 6.85 us
    psum x3 -> x0, blocking collectives: 258 us -> none  [the longest x1 126 us: body(): d_total, ff_sum = lax.psum((d_local, jnp.sum(ff_new)), ('dp', 'col'))]
    pallas_call x0 -> x1, Pallas kernels: none -> 110 us  [body(): pl.pallas_call(functools.partial(kernel, sizes, float(width * n_row), flo...]
    reduce_scatter x1 -> x0, waiting for transfers between devices: 72.7 us -> none  [body(): lax.psum_scatter(lax.dot_general(out_grad, inputs, (((0,), (0,)), ((), ()...]
    dot_general x1 -> x0, matrix products: 6.08 us -> none  [body(): lax.dot_general(out_grad, inputs, (((0,), (0,)), ((), ())), preferred_ele...]
    reduce_sum x3 -> x0, other arithmetic: 5.3 us -> none  [the longest x1 2.89 us: body(): scaled_total = lax.psum(jnp.sum(scaled * scaled), ('dp', 'row', 'col'))]
    unnamed x10 -> x12, local copies, waits for them, and re-layouts: 1.86 us -> 6.85 us
    convert_element_type x1 -> x0, other arithmetic: 3.87 us -> none  [body(): (master - LEARNING_RATE * clipped).astype(jnp.bfloat16)]
  transfers between devices with their start and end apart: 1 -> 0, of which waited for: 1 -> 0; matrix products, arithmetic and copies ran while one was open for 0% -> 0% of each run, Pallas kernels for 0% -> 0%
where the time goes in v1:
time: 119 us; the launch traced here: 118 us
  Pallas kernels  110 us (92%)
  local copies, waits for them, and re-layouts  6.85 us (6%)
    pallas_call x1, Pallas kernels, body(): pl.pallas_call(functools.partial(kernel, sizes, float(width * n_row), flo...  110 us
    unnamed x12, local copies, waits for them, and re-layouts  6.85 us

profile of v1, /device:TPU:1, one launch (start us, length us, event | category | flops | bytes accessed | tf_op | source)
XLA Modules:
  0.0 117.7 jit_solution(639716132609367104)
XLA Ops:
  0.6 0.0 copy-start
  0.6 1.3 %copy-done = bf16[768,768]{1,0:T(8,128)(2,1)S(1)} copy-done((bf16[768,768]{1,0:T(8,128)(2,1)S(1)}, bf16[768,768]{1,0:T(8,128)(2,1)}, u32[]{:S(2)}) %copy-start) | copy-done | bytes 1179672
  1.9 0.0 copy-start.1
  1.9 1.0 copy-done.1
  2.9 0.0 copy-start.2
  2.9 0.7 copy-done.2
  3.6 0.0 copy-start.3
  3.6 0.7 copy-done.3
  4.3 110.2 %shard_map.84 = (bf16[768,768]{1,0:T(8,128)(2,1)S(1)}, bf16[768,768]{1,0:T(8,128)(2,1)S(1)}, f32[6,128]{1,0:T(8,128)S(1)}, f32[6,128]{1,0:T(8,128)S(1)}) custom-call(bf16[256,768]{1,0:T(8,128)(2,1)S(1)} %copy-done.1, bf16[256,6144]{1,0:T(8,128)(2,1)} %og.1, bf16[768,768]{1,0:T(8,128)(2,1)S(1)} %copy-done, f32[6,128]{1,0:T(8,128)S(1)} %bitcast.4, ...), custom_call_target="tpu_custom_call" | custom-call | tf_op jit(solution)/shard_map/pallas_call | solution.py:180
  114.5 1.0 copy.13
  115.5 1.0 copy.14
  116.5 0.6 copy.15
  117.1 0.6 copy.16
Async XLA Ops:
  0.6 1.3 %copy-start = (bf16[768,768]{1,0:T(8,128)(2,1)S(1)}, bf16[768,768]{1,0:T(8,128)(2,1)}, u32[]{:S(2)}) copy-start(bf16[768,768]{1,0:T(8,128)(2,1)} %w_hbm.1) | copy-start | bytes 3538948
  1.9 1.0 copy-start.1
  2.9 0.7 copy-start.2
  3.6 0.7 copy-start.3

commit v2 on v1

v2 whole, which is shorter than its diff:
```python
import functools

import jax
import jax.numpy as jnp
from jax import lax
from jax.experimental import pallas as pl
from jax.experimental.pallas import tpu as pltpu
from jax.sharding import PartitionSpec as P

D = 9216
FF = 49152

DECAY_RATE = 1.0 - 10.0 ** (-0.8)
SQUARE_EPS = 1e-30
LEARNING_RATE = 0.02

MESH = pl.DeviceIdType.MESH
LANES = 128
PIECES = 3
QUARTERS = 4


def gather_kernel(sizes, d_full, ff_full, inp, og, ff_old, d_old, g_ref, ff_ref, d_ref, fac_ref,
                  a_buf, b_buf, ff_prev, d_prev, ff_buf, xy_buf, col_buf, t_buf,
                  a_send, a_recv, z_send, b_send, b_recv, y_send, c_send, c_recv, loc,
                  s_send, ff_recv, xy_recv, col_recv, t_recv):
    n_dp, n_row, n_col = sizes
    n_x = n_dp // 2
    dp, row, col = (lax.axis_index(a) for a in ("dp", "row", "col"))
    x = dp // 2
    core = dp - 2 * x
    sib = 2 * x + 1 - core
    m = lax.rem(row, PIECES)
    q = lax.rem(col, QUARTERS)
    tok, width = inp.shape
    units = g_ref.shape[0]
    piece = units // PIECES
    quarter = tok // QUARTERS
    half = quarter // 2
    blocks = units // LANES
    lane_blocks = width // LANES

    barrier = pltpu.get_barrier_semaphore()
    for axis, n, me in (("dp", n_dp, dp), ("row", n_row, row), ("col", n_col, col)):
        def greet(i, _, axis=axis, n=n, me=me):
            pl.semaphore_signal(barrier, inc=1, device_id={axis: lax.rem(me + i, n)}, device_id_type=MESH)
            return 0
        lax.fori_loop(1, n, greet, 0)

    def og_piece(to, p):
        return og.at[:, pl.ds(pl.multiple_of(to * units + p * piece, LANES), piece)]

    def rows_of(start, size):
        return pl.ds(pl.multiple_of(start, 16), size)

    own = [pltpu.make_async_copy(og_piece(dp, p), a_buf.at[p, dp], loc.at[p]) for p in range(PIECES)]
    own.append(pltpu.make_async_copy(inp, b_buf.at[dp], loc.at[3]))
    own.append(pltpu.make_async_copy(ff_old, ff_prev, loc.at[4]))
    own.append(pltpu.make_async_copy(d_old, d_prev, loc.at[5]))
    for c in own:
        c.start()

    def far(dx, flip):
        there = lax.rem(x + dx + n_x, n_x)
        return 2 * there + (1 - core if flip else core)

    def send_a(k, dx, flip):
        to = far(dx, flip)
        return pltpu.make_async_remote_copy(og_piece(to, m), a_buf.at[m, dp], a_send.at[k], a_recv.at[0, dp],
                                            device_id={"dp": to}, device_id_type=MESH)

    def send_sib_a(j):
        p = lax.rem(m + j, PIECES)
        return pltpu.make_async_remote_copy(og_piece(sib, p), a_buf.at[p, dp], c_send.at[j], a_recv.at[j, dp],
                                            device_id={"dp": sib}, device_id_type=MESH)

    def send_sib_b(k, src):
        return pltpu.make_async_remote_copy(b_buf.at[src], b_buf.at[src], c_send.at[PIECES + k], c_recv.at[src],
                                            device_id={"dp": sib}, device_id_type=MESH)

    def send_b(k, dx):
        part = rows_of(q * quarter, quarter)
        return pltpu.make_async_remote_copy(inp.at[part], b_buf.at[dp, part], b_send.at[k], b_recv.at[0, dp],
                                            device_id={"dp": far(dx, False)}, device_id_type=MESH)

    def pass_z(src, j):
        to = lax.rem(row + (n_row - 1 if j == 1 else 1), n_row)
        return pltpu.make_async_remote_copy(a_buf.at[m, src], a_buf.at[m, src], z_send.at[j - 1, src], a_recv.at[j, src],
                                            device_id={"row": to}, device_id_type=MESH)

    def pass_y(src, j):
        step = (1, -1, 2, -2)[j - 1]
        start, size = q * quarter, quarter
        if j >= 3:
            start, size = start + (j - 3) * half, half
        part = rows_of(start, size)
        return pltpu.make_async_remote_copy(b_buf.at[src, part], b_buf.at[src, part], y_send.at[j - 1, src], b_recv.at[j, src],
                                            device_id={"col": lax.rem(col + step + n_col, n_col)}, device_id_type=MESH)

    def got_a(j, src):
        p = lax.rem(m + j, PIECES)
        pltpu.make_async_remote_copy(a_buf.at[p, src], a_buf.at[p, src], a_send.at[0], a_recv.at[j, src],
                                     device_id={"dp": sib}, device_id_type=MESH).wait_recv()

    def got_b(j, src):
        shift = (0, -1, 1, -2, 2)[j]
        start, size = lax.rem(q + shift + QUARTERS, QUARTERS) * quarter, quarter
        if j >= 3:
            start, size = start + (j - 3) * half, half
        part = rows_of(start, size)
        pltpu.make_async_remote_copy(b_buf.at[src, part], b_buf.at[src, part], b_send.at[0], b_recv.at[j, src],
                                     device_id={"dp": sib}, device_id_type=MESH).wait_recv()

    def got_c(src):
        pltpu.make_async_remote_copy(b_buf.at[src], b_buf.at[src], b_send.at[0], c_recv.at[src],
                                     device_id={"dp": sib}, device_id_type=MESH).wait_recv()

    near = ((1, False), (-1, False), (1, True), (-1, True))
    away = ((2, False), (2, True))
    steps = (1, -1, 2)
    sends = [send_a(k, *t) for k, t in enumerate(near)]
    sends += [send_b(k, dx) for k, dx in enumerate(steps)]
    sends += [send_a(len(near) + k, *t) for k, t in enumerate(away)]
    sends += [send_sib_a(j) for j in range(PIECES)]

    pl.semaphore_wait(barrier, n_dp + n_row + n_col - 3)
    for c in sends:
        c.start()
    own[3].wait()
    c = send_sib_b(0, dp)
    c.start()
    sends.append(c)

    def product(j, src, first=False):
        p = lax.rem(m + j, PIECES)
        out = g_ref.at[pl.ds(pl.multiple_of(p * piece, LANES), piece)]
        value = lax.dot_general(a_buf[p, src], b_buf[src], (((0,), (0,)), ((), ())), preferred_element_type=jnp.float32)
        out[...] = value if first else out[...] + value

    for c in own[:3]:
        c.wait()
    for j in range(PIECES):
        product(j, dp, first=True)

    def relay_a(dx, flip):
        src = far(dx, flip)
        got_a(0, src)
        for j in (1, 2):
            c = pass_z(src, j)
            c.start()
            sends.append(c)

    for t in near:
        relay_a(*t)
    for dx in steps:
        src = far(dx, False)
        got_b(0, src)
        for j in (1, 2, 3, 4):
            c = pass_y(src, j)
            c.start()
            sends.append(c)
    got_c(sib)
    for j in range(PIECES):
        got_a(j, sib)
        product(j, sib)
    for t in away:
        relay_a(*t)
    for k, dx in enumerate(steps):
        src = far(dx, False)
        for j in (1, 2, 3, 4):
            got_b(j, src)
        c = send_sib_b(1 + k, src)
        c.start()
        sends.append(c)
        product(0, src)
    for dx in steps:
        src = far(dx, True)
        got_c(src)
        product(0, src)
    for t in near + away:
        src = far(*t)
        for j in (1, 2):
            got_a(j, src)
            product(j, src)

    def exchange(axis, n, me, buf, recv, meanwhile=None):
        def copy(i):
            to = lax.rem(me + i, n)
            return pltpu.make_async_remote_copy(buf.at[me], buf.at[me], s_send.at[i], recv.at[me],
                                                device_id={axis: to}, device_id_type=MESH)

        def start(i, _):
            copy(i).start()
            return 0
        lax.fori_loop(1, n, start, 0)
        if meanwhile is not None:
            meanwhile()

        def arrive(i, _):
            src = lax.rem(me + n - i, n)
            pltpu.make_async_remote_copy(buf.at[src], buf.at[src], s_send.at[0], recv.at[src],
                                         device_id={axis: src}, device_id_type=MESH).wait_recv()
            return 0
        lax.fori_loop(1, n, arrive, 0)

        def sent(i, _):
            copy(i).wait_send()
            return 0
        lax.fori_loop(1, n, sent, 0)
        total = buf[0]
        for i in range(1, n):
            total = total + buf[i]
        return total

    ff_buf[row] = jnp.zeros(ff_buf.shape[1:], jnp.float32)
    xy_buf[dp] = jnp.zeros(xy_buf.shape[1:], jnp.float32)
    d_part = [jnp.zeros((1, LANES), jnp.float32)] * lane_blocks
    for k in range(blocks):
        rows = pl.ds(k * LANES, LANES)
        part = None
        for j in range(lane_blocks):
            v = g_ref[rows, pl.ds(j * LANES, LANES)]
            sq = v * v + SQUARE_EPS
            part = sq if part is None else part + sq
            d_part[j] = d_part[j] + jnp.sum(sq, axis=0, keepdims=True)
        ff_buf[row, pl.ds(k, 1), :] = jnp.sum(part.T, axis=0, keepdims=True)
    for j in range(lane_blocks):
        xy_buf[dp, pl.ds(j, 1), :] = d_part[j]

    own[4].wait()
    own[5].wait()
    ff_total = exchange("row", n_row, row, ff_buf, ff_recv)[:blocks]
    ff_new = DECAY_RATE * ff_prev[...] + (1.0 - DECAY_RATE) * ff_total / d_full
    ff_ref[...] = ff_new
    inv = 1.0 / ff_new

    q_part = [jnp.zeros((1, LANES), jnp.float32)] * lane_blocks
    for k in range(blocks):
        rows = pl.ds(k * LANES, LANES)
        u = jnp.broadcast_to(inv[k:k + 1], (LANES, LANES)).T
        for j in range(lane_blocks):
            v = g_ref[rows, pl.ds(j * LANES, LANES)]
            q_part[j] = q_part[j] + jnp.sum(v * v * u, axis=0, keepdims=True)
    for j in range(lane_blocks):
        xy_buf[dp, pl.ds(lane_blocks + j, 1), :] = q_part[j]
    xy_buf[dp, pl.ds(2 * lane_blocks, 1), :] = jnp.sum(ff_new, axis=0, keepdims=True)

    col_buf[col] = exchange("dp", n_dp, dp, xy_buf, xy_recv)
    total = exchange("col", n_col, col, col_buf, col_recv)
    d_new = DECAY_RATE * d_prev[...] + (1.0 - DECAY_RATE) * total[:lane_blocks] / ff_full
    d_ref[...] = d_new
    ff_mean = jnp.sum(total[2 * lane_blocks:2 * lane_blocks + 1], axis=1, keepdims=True) / ff_full
    t_buf[row] = jnp.zeros(t_buf.shape[1:], jnp.float32)
    t_buf[row, pl.ds(0, lane_blocks), :] = total[lane_blocks:2 * lane_blocks] / d_new
    inv_d = lax.rsqrt(d_new)
    inv_f = lax.rsqrt(ff_new)

    def scale():
        for k in range(blocks):
            rows = pl.ds(k * LANES, LANES)
            u = jnp.broadcast_to(inv_f[k:k + 1], (LANES, LANES)).T
            for j in range(lane_blocks):
                cols = pl.ds(j * LANES, LANES)
                g_ref[rows, cols] = g_ref[rows, cols] * u * inv_d[j:j + 1]

    t_total = exchange("row", n_row, row, t_buf, t_recv, scale)
    square_mean = jnp.sum(jnp.sum(t_total, axis=0, keepdims=True), axis=1, keepdims=True) * ff_mean / (d_full * ff_full)
    factor = jnp.sqrt(ff_mean) / jnp.maximum(1.0, jnp.sqrt(square_mean))
    fac_ref[...] = jnp.broadcast_to(factor, fac_ref.shape)
    for c in sends:
        c.wait_send()


def write_kernel(g, fac, w, ff_in, d_in, upd, new, ff_out, d_out, upd_buf, new_buf, sem):
    copies = [pltpu.make_async_copy(ff_in, ff_out, sem.at[0, 0]), pltpu.make_async_copy(d_in, d_out, sem.at[1, 0])]
    for c in copies:
        c.start()
    factor = fac[0:1, 0:1]
    for k in range(g.shape[0] // LANES):
        rows = pl.ds(k * LANES, LANES)
        clipped = g[rows, :] * factor
        upd_buf[rows, :] = clipped.astype(jnp.bfloat16)
        new_buf[rows, :] = (w[rows, :].astype(jnp.float32) - LEARNING_RATE * clipped).astype(jnp.bfloat16)
        for i, (src, dst) in enumerate(((upd_buf, upd), (new_buf, new))):
            c = pltpu.make_async_copy(src.at[rows], dst.at[rows], sem.at[i, k + 1])
            c.start()
            copies.append(c)
    for c in copies:
        c.wait()


def solution(mesh):
    sizes = n_dp, n_row, n_col = tuple(mesh.shape[a] for a in ("dp", "row", "col"))

    def body(inputs, out_grad, weight, ff_old, d_old):
        tok, width = inputs.shape
        units = weight.shape[0]
        hbm = pl.BlockSpec(memory_space=pltpu.HBM)
        vmem = pl.BlockSpec(memory_space=pltpu.VMEM)
        f32, bf16 = jnp.float32, jnp.bfloat16
        fr, dr = units // LANES, width // LANES
        dma = pltpu.SemaphoreType.DMA
        shape = jax.ShapeDtypeStruct
        g, ff_new, d_new, fac = pl.pallas_call(
            functools.partial(gather_kernel, sizes, float(width * n_row), float(units * n_dp * n_col)),
            out_shape=(shape((units, width), f32), shape((fr, LANES), f32), shape((dr, LANES), f32), shape((8, LANES), f32)),
            in_specs=[hbm] * 4,
            out_specs=(vmem,) * 4,
            scratch_shapes=[
                pltpu.VMEM((PIECES, n_dp, tok, units // PIECES), bf16),
                pltpu.VMEM((n_dp, tok, width), bf16),
                pltpu.VMEM((fr, LANES), f32),
                pltpu.VMEM((dr, LANES), f32),
                pltpu.VMEM((n_row, 8, LANES), f32),
                pltpu.VMEM((n_dp, 16, LANES), f32),
                pltpu.VMEM((n_col, 16, LANES), f32),
                pltpu.VMEM((n_row, 8, LANES), f32),
                dma((6,)), dma((PIECES, n_dp)), dma((2, n_dp)),
                dma((3,)), dma((5, n_dp)), dma((4, n_dp)),
                dma((PIECES + 4,)), dma((n_dp,)), dma((6,)),
                dma((max(sizes),)), dma((n_row,)), dma((n_dp,)), dma((n_col,)), dma((n_row,)),
            ],
            compiler_params=pltpu.CompilerParams(collective_id=0, has_side_effects=True, vmem_limit_bytes=51 * 2**20),
            name="gather_product_stats",
        )(inputs, out_grad, ff_old.reshape(fr, LANES), d_old.reshape(dr, LANES))
        upd, new, ff_out, d_out = pl.pallas_call(
            write_kernel,
            out_shape=(shape((units, width), bf16), shape((units, width), bf16), shape((fr, LANES), f32), shape((dr, LANES), f32)),
            in_specs=[vmem] * 5,
            out_specs=(hbm,) * 4,
            scratch_shapes=[
                pltpu.VMEM((units, width), bf16),
                pltpu.VMEM((units, width), bf16),
                dma((2, fr + 1)),
            ],
            compiler_params=pltpu.CompilerParams(vmem_limit_bytes=40 * 2**20),
            name="write_results",
        )(g, fac, weight, ff_new, d_new)
        return upd, new, ff_out.reshape(units), d_out.reshape(width)

    return jax.shard_map(
        body,
        mesh=mesh,
        in_specs=(
            P("dp", "row"),
            P("dp", "col"),
            P(("col", "dp"), "row"),
            P(("col", "dp")),
            P("row"),
        ),
        out_specs=(P(("col", "dp"), "row"), P(("col", "dp"), "row"), P(("col", "dp")), P("row")),
        check_vma=False,
    )
```

time: 119 us -> 75.6 us (0.64)
  Pallas kernels: 110 us -> 72.3 us
  local copies, waits for them, and re-layouts: 6.85 us -> 2.37 us
    pallas_call x1 -> x2, Pallas kernels: 110 us -> 72.3 us  [the longest x1 70.7 us: body(): pl.pallas_call(functools.partial(gather_kernel, sizes, float(width * n_ro...]
    unnamed x12 -> x8, local copies, waits for them, and re-layouts: 6.85 us -> 2.37 us
where the time goes in v2:
time: 75.6 us; the launch traced here: 75.4 us
  Pallas kernels  72.3 us (96%)
  local copies, waits for them, and re-layouts  2.37 us (3%)
    pallas_call x1, Pallas kernels, body(): pl.pallas_call(functools.partial(gather_kernel, sizes, float(width * n_ro...  70.7 us
    unnamed x8, local copies, waits for them, and re-layouts  2.37 us
    pallas_call x1, Pallas kernels, body(): pl.pallas_call(write_kernel, out_shape=(shape((units, width), bf16), shap...  1.59 us

profile of v2, /device:TPU:1, one launch (start us, length us, event | category | flops | bytes accessed | tf_op | source)
XLA Modules:
  0.0 75.4 jit_solution(16293849139228353422)
XLA Ops:
  0.6 0.0 copy-start.1
  0.6 1.0 %copy-done.1 = bf16[256,768]{1,0:T(8,128)(2,1)S(1)} copy-done((bf16[256,768]{1,0:T(8,128)(2,1)S(1)}, bf16[256,768]{1,0:T(8,128)(2,1)}, u32[]{:S(2)}) %copy-start.1) | copy-done | bytes 393240
  1.6 0.0 copy-start.2
  1.6 0.7 copy-done.2
  2.3 0.0 copy-start.3
  2.3 0.7 copy-done.3
  3.0 0.0 copy-start
  3.0 70.7 %gather_product_stats.1 = (f32[768,768]{1,0:T(8,128)S(1)}, f32[6,128]{1,0:T(8,128)S(1)}, f32[6,128]{1,0:T(8,128)S(1)}, f32[8,128]{1,0:T(8,128)S(1)}) custom-call(bf16[256,768]{1,0:T(8,128)(2,1)S(1)} %copy-done.1, bf16[256,6144]{1,0:T(8,128)(2,1)} %og.1, f32[6,128]{1,0:T(8,128)S(1)} %bitcast.4, f32[6,128]{1,0:T(8,128)S(1)} %bitcast.5), custom_call_target="tpu_custom_call" | custom-call | tf_op jit(solution)/shard_map/gather_product_stats/pallas_call | solution.py:304
  73.8 0.0 copy-done
  73.8 1.6 %write_results.1 = (bf16[768,768]{1,0:T(8,128)(2,1)}, bf16[768,768]{1,0:T(8,128)(2,1)}, f32[6,128]{1,0:T(8,128)}, f32[6,128]{1,0:T(8,128)}) custom-call(f32[768,768]{1,0:T(8,128)S(1)} %get-tuple-element.12.g, f32[8,128]{1,0:T(8,128)S(1)} %get-tuple-element.13.fac, bf16[768,768]{1,0:T(8,128)(2,1)S(1)} %copy-done, f32[6,128]{1,0:T(8,128)S(1)} %get-tuple-element.14.ff_in, ...), custom_call_target="tpu_custom_call" | custom-call | tf_op jit(solution)/shard_map/write_results/pallas_call | solution.py:326
Async XLA Ops:
  0.6 1.0 %copy-start.1 = (bf16[256,768]{1,0:T(8,128)(2,1)S(1)}, bf16[256,768]{1,0:T(8,128)(2,1)}, u32[]{:S(2)}) copy-start(bf16[256,768]{1,0:T(8,128)(2,1)} %inp.1) | copy-start | bytes 1179652
  1.6 0.7 copy-start.2
  2.3 0.7 copy-start.3
  3.0 70.8 %copy-start = (bf16[768,768]{1,0:T(8,128)(2,1)S(1)}, bf16[768,768]{1,0:T(8,128)(2,1)}, u32[]{:S(2)}) copy-start(bf16[768,768]{1,0:T(8,128)(2,1)} %w.1) | copy-start | bytes 3538948

commit v3 on v2

v3 whole, which is shorter than its diff:
```python
import functools

import jax
import jax.numpy as jnp
from jax import lax
from jax.experimental import pallas as pl
from jax.experimental.pallas import tpu as pltpu
from jax.sharding import PartitionSpec as P

D = 9216
FF = 49152

DECAY_RATE = 1.0 - 10.0 ** (-0.8)
SQUARE_EPS = 1e-30
LEARNING_RATE = 0.02

MESH = pl.DeviceIdType.MESH
LANES = 128
PIECES = 3
QUARTERS = 4


def gather_kernel(sizes, d_full, ff_full, inp, og, ff_old, d_old, g_out, ff_out, d_out, fac_out,
                  g_ref, a_buf, b_buf, ff_prev, d_prev, ff_res, d_res, fac_res, ff_buf, d_buf, dcol_buf, q_buf, xy_buf, t_buf,
                  a_send, a_recv, z_send, b_send, b_recv, y_send, c_send, sib_send, c_recv, loc, out_sem,
                  ff_sems, d_sems, dcol_sems, xy_sems, t_sems, heard):
    n_dp, n_row, n_col = sizes
    n_x = n_dp // 2
    dp, row, col = (lax.axis_index(a) for a in ("dp", "row", "col"))
    x = dp // 2
    core = dp - 2 * x
    sib = 2 * x + 1 - core
    m = lax.rem(row, PIECES)
    q = lax.rem(col, QUARTERS)
    tok, width = inp.shape
    units = g_ref.shape[0]
    piece = units // PIECES
    quarter = tok // QUARTERS
    half = quarter // 2
    blocks = units // LANES
    lane_blocks = width // LANES

    barrier = pltpu.get_barrier_semaphore()
    def others(axis, n, me):
        order = sorted(range(1, n), key=lambda t: -min(t, n - t))
        return [{axis: lax.rem(me + t, n)} for t in order]

    rows_far, cols_far, dps_far = others("row", n_row, row), others("col", n_col, col), others("dp", n_dp, dp)
    greeted = rows_far[-2:] + cols_far[-4:] + dps_far
    for there in greeted:
        pl.semaphore_signal(barrier, inc=1, device_id=there, device_id_type=MESH)

    def og_piece(to, p):
        return og.at[:, pl.ds(pl.multiple_of(to * units + p * piece, LANES), piece)]

    def rows_of(start, size):
        return pl.ds(pl.multiple_of(start, 16), size)

    own = [pltpu.make_async_copy(og_piece(dp, p), a_buf.at[p, dp], loc.at[p]) for p in range(PIECES)]
    own.append(pltpu.make_async_copy(inp, b_buf.at[dp], loc.at[3]))
    own.append(pltpu.make_async_copy(ff_old, ff_prev, loc.at[4]))
    own.append(pltpu.make_async_copy(d_old, d_prev, loc.at[5]))
    for c in own:
        c.start()

    def far(dx, flip):
        there = lax.rem(x + dx + n_x, n_x)
        return 2 * there + (1 - core if flip else core)

    def send_a(k, dx, flip):
        to = far(dx, flip)
        return pltpu.make_async_remote_copy(og_piece(to, m), a_buf.at[m, dp], a_send.at[k], a_recv.at[0, dp],
                                            device_id={"dp": to}, device_id_type=MESH)

    def send_sib_a(j):
        p = lax.rem(m + j, PIECES)
        return pltpu.make_async_remote_copy(og_piece(sib, p), a_buf.at[p, dp], sib_send.at[j], a_recv.at[j, dp],
                                            device_id={"dp": sib}, device_id_type=MESH)

    def send_b(k, dx):
        part = rows_of(q * quarter, quarter)
        return pltpu.make_async_remote_copy(inp.at[part], b_buf.at[dp, part], b_send.at[k], b_recv.at[0, dp],
                                            device_id={"dp": far(dx, False)}, device_id_type=MESH)

    def pass_z(src, j):
        to = lax.rem(row + (n_row - 1 if j == 1 else 1), n_row)
        return pltpu.make_async_remote_copy(a_buf.at[m, src], a_buf.at[m, src], z_send.at[j - 1, src], a_recv.at[j, src],
                                            device_id={"row": to}, device_id_type=MESH)

    def pass_y(src, j):
        step = (1, -1, 2, -2)[j - 1]
        start, size = q * quarter, quarter
        if j >= 3:
            start, size = start + (j - 3) * half, half
        part = rows_of(start, size)
        return pltpu.make_async_remote_copy(b_buf.at[src, part], b_buf.at[src, part], y_send.at[j - 1, src], b_recv.at[j, src],
                                            device_id={"col": lax.rem(col + step + n_col, n_col)}, device_id_type=MESH)

    def part_of(j):
        shift = (0, -1, 1, -2, 2)[j]
        start, size = lax.rem(q + shift + QUARTERS, QUARTERS) * quarter, quarter
        if j >= 3:
            start, size = start + (j - 3) * half, half
        return rows_of(start, size)

    def share(src, j):
        part = part_of(j)
        return pltpu.make_async_remote_copy(b_buf.at[src, part], b_buf.at[src, part], c_send.at[j, src], c_recv.at[j, src],
                                            device_id={"dp": sib}, device_id_type=MESH)

    def got_a(j, src):
        p = lax.rem(m + j, PIECES)
        pltpu.make_async_remote_copy(a_buf.at[p, src], a_buf.at[p, src], a_send.at[0], a_recv.at[j, src],
                                     device_id={"dp": sib}, device_id_type=MESH).wait_recv()

    def got_b(j, src, recv):
        part = part_of(j)
        pltpu.make_async_remote_copy(b_buf.at[src, part], b_buf.at[src, part], b_send.at[0], recv.at[j, src],
                                     device_id={"dp": sib}, device_id_type=MESH).wait_recv()

    near = ((1, False), (-1, False), (1, True), (-1, True))
    away = ((2, False), (2, True))
    steps = (1, -1, 2)
    order = ("n0", "n1", "b0", "b1", "n2", "n3", "w0", "b2", "w1")
    moves = {}
    for k, t in enumerate(near):
        moves["n" + str(k)] = send_a(k, *t)
    for k, t in enumerate(away):
        moves["w" + str(k)] = send_a(len(near) + k, *t)
    for k, dx in enumerate(steps):
        moves["b" + str(k)] = send_b(k, dx)
    sends = [moves[k] for k in order]
    sends += [send_sib_a(j) for j in range(PIECES)]

    pl.semaphore_wait(barrier, len(greeted))

    def hail():
        for i, there in enumerate(rows_far[-2:]):
            pl.semaphore_signal(heard.at[i], inc=1, device_id=there, device_id_type=MESH)

    def answered():
        for i in range(2):
            pl.semaphore_wait(heard.at[i], 1)

    hail()
    for c in sends:
        c.start()

    def go(c):
        c.start()
        sends.append(c)

    own[3].wait()
    go(pltpu.make_async_remote_copy(b_buf.at[dp], b_buf.at[dp], sib_send.at[PIECES], c_recv.at[0, dp],
                                    device_id={"dp": sib}, device_id_type=MESH))

    def product(j, chip, first=False):
        p = lax.rem(m + j, PIECES)
        out = g_ref.at[pl.ds(pl.multiple_of(p * piece, LANES), piece)]
        pair = pl.ds(2 * chip, 2)
        value = lax.dot_general(a_buf[p, pair].reshape(2 * tok, piece), b_buf[pair].reshape(2 * tok, width),
                                (((0,), (0,)), ((), ())), preferred_element_type=jnp.float32)
        out[...] = value if first else out[...] + value

    def relay_a(dx, flip):
        src = far(dx, flip)
        got_a(0, src)
        go(pass_z(src, 1))
        go(pass_z(src, 2))

    def relay_b(dx):
        src = far(dx, False)
        got_b(0, src, b_recv)
        for j in (1, 2, 3, 4):
            go(pass_y(src, j))
        go(share(src, 0))

    def collect_b(dx):
        src = far(dx, False)
        for j in (1, 2, 3, 4):
            got_b(j, src, b_recv)
            go(share(src, j))

    def take(dx, j):
        got_a(j, far(dx, False)) if j else None
        got_a(j, far(dx, True)) if j else None
        product(j, lax.rem(x + dx + n_x, n_x))

    def relay(name):
        k = int(name[1])
        if name[0] == "b":
            relay_b(steps[k])
        else:
            relay_a(*(near if name[0] == "n" else away)[k])

    for k, name in enumerate(order[:-2]):
        relay(name)
        if k in (1, 4, 6):
            answered()
            hail()
    for c in own[:3]:
        c.wait()
    pltpu.make_async_remote_copy(b_buf.at[sib], b_buf.at[sib], b_send.at[0], c_recv.at[0, sib],
                                 device_id={"dp": sib}, device_id_type=MESH).wait_recv()
    for j in range(PIECES):
        got_a(j, sib)
        product(j, x, first=True)
    collect_b(steps[0])
    relay(order[-2])
    collect_b(steps[1])
    answered()
    hail()
    relay(order[-1])
    collect_b(steps[2])
    answered()
    own[4].wait()
    own[5].wait()

    d_part = [jnp.zeros((8, LANES), jnp.float32)] * lane_blocks

    def squares(j):
        p = lax.rem(m + j, PIECES)
        for i in range(piece // LANES):
            rows = pl.ds(pl.multiple_of(p * piece, LANES) + i * LANES, LANES)
            part = None
            for k in range(lane_blocks):
                v = g_ref[rows, pl.ds(k * LANES, LANES)]
                sq = v * v + SQUARE_EPS
                part = sq if part is None else part + sq
                d_part[k] = d_part[k] + jnp.sum(sq.reshape(LANES // 8, 8, LANES), axis=0)
            ff_buf[row, pl.ds(p * (piece // LANES) + i, 1), :] = jnp.sum(part.T, axis=0, keepdims=True)

    for dx in steps:
        for j in range(5):
            got_b(j, far(dx, True), c_recv)
        for j in range(PIECES):
            take(dx, j)
            if dx == steps[-1]:
                squares(j)
    for k in range(lane_blocks):
        d_buf[dp, pl.ds(k, 1), :] = jnp.sum(d_part[k], axis=0, keepdims=True)

    def spread(buf, me, sems, targets):
        for there in targets:
            pltpu.make_async_remote_copy(buf.at[me], buf.at[me], sems.at[0], sems.at[1],
                                         device_id=there, device_id_type=MESH).start()

    def slots(buf, sems):
        rest = buf.at[pl.ds(0, buf.shape[0] - 1)]
        return pltpu.make_async_remote_copy(rest, rest, sems.at[0], sems.at[1], device_id={"dp": sib}, device_id_type=MESH)

    def collect(buf, sems):
        slots(buf, sems).wait_recv()
        terms = [buf[k] for k in range(buf.shape[0])]
        while len(terms) > 1:
            terms = [sum(terms[k + 1:k + 2], terms[k]) for k in range(0, len(terms), 2)]
        return terms[0]

    outs = []

    def put(src, dst, k):
        c = pltpu.make_async_copy(src, dst, out_sem.at[k])
        c.start()
        outs.append(c)

    spread(d_buf, dp, d_sems, dps_far)
    spread(ff_buf, row, ff_sems, rows_far)
    dcol_buf[col] = collect(d_buf, d_sems)
    spread(dcol_buf, col, dcol_sems, cols_far)
    ff_new = DECAY_RATE * ff_prev[...] + (1.0 - DECAY_RATE) * collect(ff_buf, ff_sems) / d_full
    ff_res[...] = ff_new
    put(ff_res, ff_out, blocks)
    inv = 1.0 / ff_new

    q_part = [jnp.zeros((8, LANES), jnp.float32)] * lane_blocks
    for k in range(blocks):
        rows = pl.ds(k * LANES, LANES)
        u = jnp.broadcast_to(inv[k:k + 1], (LANES, LANES)).T
        for j in range(lane_blocks):
            v = g_ref[rows, pl.ds(j * LANES, LANES)]
            q_part[j] = q_part[j] + jnp.sum((v * v * u).reshape(LANES // 8, 8, LANES), axis=0)
    for j in range(lane_blocks):
        q_buf[pl.ds(j, 1), :] = jnp.sum(q_part[j], axis=0, keepdims=True)

    d_new = DECAY_RATE * d_prev[...] + (1.0 - DECAY_RATE) * collect(dcol_buf, dcol_sems) / ff_full
    d_res[...] = d_new
    put(d_res, d_out, blocks + 1)

    def whole(v):
        return jnp.sum(jnp.sum(v, axis=0, keepdims=True), axis=1, keepdims=True)

    here = col * n_dp + dp
    lane = lax.broadcasted_iota(jnp.int32, (1, LANES), 1)
    xy_buf[here] = jnp.where(lane < LANES // 2, whole(q_buf[...] / d_new), whole(ff_new))
    spread(xy_buf, here, xy_sems, [{**c, **d} for c in cols_far + [{"col": col}] for d in dps_far + [{"dp": dp}]][:-1])
    total = collect(xy_buf, xy_sems)
    ff_mean = total[:, LANES - 1:] / ff_full
    t_buf[row] = total
    inv_d = lax.rsqrt(d_new)
    inv_f = lax.rsqrt(ff_new)

    def scale():
        for k in range(blocks):
            rows = pl.ds(k * LANES, LANES)
            u = jnp.broadcast_to(inv_f[k:k + 1], (LANES, LANES)).T
            for j in range(lane_blocks):
                cols = pl.ds(j * LANES, LANES)
                g_ref[rows, cols] = g_ref[rows, cols] * u * inv_d[j:j + 1]
            put(g_ref.at[rows], g_out.at[rows], k)

    spread(t_buf, row, t_sems, rows_far)
    scale()
    for c in sends:
        c.wait_send()
    for buf, sems in ((ff_buf, ff_sems), (d_buf, d_sems), (dcol_buf, dcol_sems), (xy_buf, xy_sems)):
        slots(buf, sems).wait_send()
    for c in outs:
        c.wait()
    t_total = collect(t_buf, t_sems)
    square_mean = t_total[:, :1] * ff_mean / (d_full * ff_full)
    factor = jnp.sqrt(ff_mean) / jnp.maximum(1.0, jnp.sqrt(square_mean))
    fac_res[...] = jnp.broadcast_to(factor, fac_res.shape)
    put(fac_res, fac_out, blocks + 2)
    slots(t_buf, t_sems).wait_send()
    outs[-1].wait()


def write_kernel(g, fac, w, ff_in, d_in, upd, new, ff_out, d_out, g_buf, fac_buf, w_buf, upd_buf, new_buf, in_sem, out_sem):
    n = g.shape[0] // LANES
    chunk = [pl.ds(k * LANES, LANES) for k in range(n)]
    loads = [pltpu.make_async_copy(fac, fac_buf, in_sem.at[0, n])]
    for k, rows in enumerate(chunk):
        loads.append(pltpu.make_async_copy(g.at[rows], g_buf.at[rows], in_sem.at[0, k]))
        loads.append(pltpu.make_async_copy(w.at[rows], w_buf.at[rows], in_sem.at[1, k]))
    for c in loads:
        c.start()
    loads[0].wait()
    factor = fac_buf[0:1, 0:1]
    copies = [pltpu.make_async_copy(ff_in, ff_out, out_sem.at[0, n]), pltpu.make_async_copy(d_in, d_out, out_sem.at[1, n])]
    for c in copies:
        c.start()
    for k, rows in enumerate(chunk):
        loads[2 * k + 1].wait()
        loads[2 * k + 2].wait()
        clipped = g_buf[rows, :] * factor
        upd_buf[rows, :] = clipped.astype(jnp.bfloat16)
        new_buf[rows, :] = (w_buf[rows, :].astype(jnp.float32) - LEARNING_RATE * clipped).astype(jnp.bfloat16)
        for i, (src, dst) in enumerate(((upd_buf, upd), (new_buf, new))):
            c = pltpu.make_async_copy(src.at[rows], dst.at[rows], out_sem.at[i, k])
            c.start()
            copies.append(c)
    for c in copies:
        c.wait()


def solution(mesh):
    sizes = n_dp, n_row, n_col = tuple(mesh.shape[a] for a in ("dp", "row", "col"))

    def body(inputs, out_grad, weight, ff_old, d_old):
        tok, width = inputs.shape
        units = weight.shape[0]
        hbm = pl.BlockSpec(memory_space=pltpu.HBM)
        f32, bf16 = jnp.float32, jnp.bfloat16
        fr, dr = units // LANES, width // LANES
        dma = pltpu.SemaphoreType.DMA
        shape, vmem = jax.ShapeDtypeStruct, pltpu.VMEM
        g, ff_new, d_new, fac = pl.pallas_call(
            functools.partial(gather_kernel, sizes, float(width * n_row), float(units * n_dp * n_col)),
            out_shape=(shape((units, width), f32), shape((fr, LANES), f32), shape((dr, LANES), f32), shape((8, LANES), f32)),
            in_specs=[hbm] * 4,
            out_specs=(hbm,) * 4,
            scratch_shapes=[
                vmem((units, width), f32),
                vmem((PIECES, n_dp, tok, units // PIECES), bf16),
                vmem((n_dp, tok, width), bf16),
                vmem((fr, LANES), f32),
                vmem((dr, LANES), f32),
                vmem((fr, LANES), f32),
                vmem((dr, LANES), f32),
                vmem((8, LANES), f32),
                vmem((n_row, fr, LANES), f32),
                vmem((n_dp, dr, LANES), f32),
                vmem((n_col, dr, LANES), f32),
                vmem((dr, LANES), f32),
                vmem((n_dp * n_col, 1, LANES), f32),
                vmem((n_row, 1, LANES), f32),
                dma((6,)), dma((PIECES, n_dp)), dma((2, n_dp)),
                dma((3,)), dma((5, n_dp)), dma((4, n_dp)),
                dma((5, n_dp)), dma((PIECES + 1,)), dma((5, n_dp)), dma((6,)), dma((fr + 3,)),
                dma((2,)), dma((2,)), dma((2,)), dma((2,)), dma((2,)),
                pltpu.SemaphoreType.REGULAR((2,)),
            ],
            compiler_params=pltpu.CompilerParams(collective_id=0, has_side_effects=True, vmem_limit_bytes=56 * 2**20),
            name="gather_product_stats",
        )(inputs, out_grad, ff_old.reshape(fr, LANES), d_old.reshape(dr, LANES))
        upd, new, ff_res, d_res = pl.pallas_call(
            write_kernel,
            out_shape=(shape((units, width), bf16), shape((units, width), bf16), shape((fr, LANES), f32), shape((dr, LANES), f32)),
            in_specs=[hbm] * 5,
            out_specs=(hbm,) * 4,
            scratch_shapes=[
                vmem((units, width), f32),
                vmem((8, LANES), f32),
                vmem((units, width), bf16),
                vmem((units, width), bf16),
                vmem((units, width), bf16),
                dma((2, fr + 1)),
                dma((2, fr + 1)),
            ],
            compiler_params=pltpu.CompilerParams(vmem_limit_bytes=56 * 2**20),
            name="write_results",
        )(g, fac, weight, ff_new, d_new)
        return upd, new, ff_res.reshape(units), d_res.reshape(width)

    return jax.shard_map(
        body,
        mesh=mesh,
        in_specs=(
            P("dp", "row"),
            P("dp", "col"),
            P(("col", "dp"), "row"),
            P(("col", "dp")),
            P("row"),
        ),
        out_specs=(P(("col", "dp"), "row"), P(("col", "dp"), "row"), P(("col", "dp")), P("row")),
        check_vma=False,
    )
```

time: 75.6 us -> 68.8 us (0.910)
  Pallas kernels: 72.3 us -> 68 us
  local copies, waits for them, and re-layouts: 2.37 us -> 0 us
    pallas_call x1, Pallas kernels: 70.7 us -> 65 us  [body(): pl.pallas_call(functools.partial(gather_kernel, sizes, float(width * n_ro...]
    unnamed x8 -> x0, local copies, waits for them, and re-layouts: 2.37 us -> none
    pallas_call x1, Pallas kernels: 1.59 us -> 2.99 us  [body(): pl.pallas_call(write_kernel, out_shape=(shape((units, width), bf16), shap...]
where the time goes in v3:
time: 68.8 us; the launch traced here: 68.7 us
  Pallas kernels  68 us (99%)
    pallas_call x1, Pallas kernels, body(): pl.pallas_call(functools.partial(gather_kernel, sizes, float(width * n_ro...  65 us
    pallas_call x1, Pallas kernels, body(): pl.pallas_call(write_kernel, out_shape=(shape((units, width), bf16), shap...  2.99 us

profile of v3, /device:TPU:1, one launch (start us, length us, event | category | flops | bytes accessed | tf_op | source)
XLA Modules:
  0.0 68.7 jit_solution(10556700487049608398)
XLA Ops:
  0.6 65.0 %gather_product_stats.1 = (f32[768,768]{1,0:T(8,128)}, f32[6,128]{1,0:T(8,128)}, f32[6,128]{1,0:T(8,128)}, f32[8,128]{1,0:T(8,128)}) custom-call(bf16[256,768]{1,0:T(8,128)(2,1)} %inp.1, bf16[256,6144]{1,0:T(8,128)(2,1)} %og.1, f32[6,128]{1,0:T(8,128)} %bitcast.4, f32[6,128]{1,0:T(8,128)} %bitcast.5), custom_call_target="tpu_custom_call" | custom-call | tf_op jit(solution)/shard_map/gather_product_stats/pallas_call | solution.py:367
  65.7 3.0 %write_results.1 = (bf16[768,768]{1,0:T(8,128)(2,1)}, bf16[768,768]{1,0:T(8,128)(2,1)}, f32[6,128]{1,0:T(8,128)}, f32[6,128]{1,0:T(8,128)}) custom-call(f32[768,768]{1,0:T(8,128)} %get-tuple-element.12.g, f32[8,128]{1,0:T(8,128)} %get-tuple-element.13.fac, bf16[768,768]{1,0:T(8,128)(2,1)} %w.1, f32[6,128]{1,0:T(8,128)} %get-tuple-element.14.ff_in, ...), custom_call_target="tpu_custom_call" | custom-call | tf_op jit(solution)/shard_map/write_results/pallas_call | solution.py:396

commit v4 on v3

--- a/solution.py
+++ b/solution.py
@@ -16,6 +16,7 @@
 
 MESH = pl.DeviceIdType.MESH
 LANES = 128
+CHUNK = 256
 PIECES = 3
 QUARTERS = 4
 
@@ -205,14 +206,6 @@
     for j in range(PIECES):
         got_a(j, sib)
         product(j, x, first=True)
-    collect_b(steps[0])
-    relay(order[-2])
-    collect_b(steps[1])
-    answered()
-    hail()
-    relay(order[-1])
-    collect_b(steps[2])
-    answered()
     own[4].wait()
     own[5].wait()
 
@@ -230,13 +223,25 @@
                 d_part[k] = d_part[k] + jnp.sum(sq.reshape(LANES // 8, 8, LANES), axis=0)
             ff_buf[row, pl.ds(p * (piece // LANES) + i, 1), :] = jnp.sum(part.T, axis=0, keepdims=True)
 
-    for dx in steps:
+    def takes(dx):
         for j in range(5):
             got_b(j, far(dx, True), c_recv)
         for j in range(PIECES):
             take(dx, j)
             if dx == steps[-1]:
                 squares(j)
+
+    collect_b(steps[0])
+    relay(order[-2])
+    collect_b(steps[1])
+    answered()
+    hail()
+    takes(steps[0])
+    relay(order[-1])
+    takes(steps[1])
+    collect_b(steps[2])
+    answered()
+    takes(steps[2])
     for k in range(lane_blocks):
         d_buf[dp, pl.ds(k, 1), :] = jnp.sum(d_part[k], axis=0, keepdims=True)
 
@@ -326,19 +331,19 @@
 
 
 def write_kernel(g, fac, w, ff_in, d_in, upd, new, ff_out, d_out, g_buf, fac_buf, w_buf, upd_buf, new_buf, in_sem, out_sem):
-    n = g.shape[0] // LANES
-    chunk = [pl.ds(k * LANES, LANES) for k in range(n)]
+    n = g.shape[0] // CHUNK
+    chunk = [pl.ds(k * CHUNK, CHUNK) for k in range(n)]
     loads = [pltpu.make_async_copy(fac, fac_buf, in_sem.at[0, n])]
     for k, rows in enumerate(chunk):
         loads.append(pltpu.make_async_copy(g.at[rows], g_buf.at[rows], in_sem.at[0, k]))
         loads.append(pltpu.make_async_copy(w.at[rows], w_buf.at[rows], in_sem.at[1, k]))
     for c in loads:
         c.start()
+    copies = [pltpu.make_async_copy(ff_in, ff_out, out_sem.at[0, n]), pltpu.make_async_copy(d_in, d_out, out_sem.at[1, n])]
+    for c in copies:
+        c.start()
     loads[0].wait()
     factor = fac_buf[0:1, 0:1]
-    copies = [pltpu.make_async_copy(ff_in, ff_out, out_sem.at[0, n]), pltpu.make_async_copy(d_in, d_out, out_sem.at[1, n])]
-    for c in copies:
-        c.start()
     for k, rows in enumerate(chunk):
         loads[2 * k + 1].wait()
         loads[2 * k + 2].wait()
@@ -404,8 +409,8 @@
                 vmem((units, width), bf16),
                 vmem((units, width), bf16),
                 vmem((units, width), bf16),
-                dma((2, fr + 1)),
-                dma((2, fr + 1)),
+                dma((2, units // CHUNK + 1)),
+                dma((2, units // CHUNK + 1)),
             ],
             compiler_params=pltpu.CompilerParams(vmem_limit_bytes=56 * 2**20),
             name="write_results",

time: 68.8 us -> 67.3 us (0.978)
  Pallas kernels: 68 us -> 66.6 us
    pallas_call x1, Pallas kernels: 65 us -> 63.5 us  [body(): pl.pallas_call(functools.partial(gather_kernel, sizes, float(width * n_ro...]
where the time goes in v4:
time: 67.3 us; the launch traced here: 67.2 us
  Pallas kernels  66.6 us (99%)
    pallas_call x1, Pallas kernels, body(): pl.pallas_call(functools.partial(gather_kernel, sizes, float(width * n_ro...  63.5 us
    pallas_call x1, Pallas kernels, body(): pl.pallas_call(write_kernel, out_shape=(shape((units, width), bf16), shap...  3.03 us

profile of v4, /device:TPU:1, one launch (start us, length us, event | category | flops | bytes accessed | tf_op | source)
XLA Modules:
  0.0 67.2 jit_solution(10756497978070514881)
XLA Ops:
  0.6 63.5 %gather_product_stats.1 = (f32[768,768]{1,0:T(8,128)}, f32[6,128]{1,0:T(8,128)}, f32[6,128]{1,0:T(8,128)}, f32[8,128]{1,0:T(8,128)}) custom-call(bf16[256,768]{1,0:T(8,128)(2,1)} %inp.1, bf16[256,6144]{1,0:T(8,128)(2,1)} %og.1, f32[6,128]{1,0:T(8,128)} %bitcast.4, f32[6,128]{1,0:T(8,128)} %bitcast.5), custom_call_target="tpu_custom_call" | custom-call | tf_op jit(solution)/shard_map/gather_product_stats/pallas_call | solution.py:372
  64.2 3.0 %write_results.1 = (bf16[768,768]{1,0:T(8,128)(2,1)}, bf16[768,768]{1,0:T(8,128)(2,1)}, f32[6,128]{1,0:T(8,128)}, f32[6,128]{1,0:T(8,128)}) custom-call(f32[768,768]{1,0:T(8,128)} %get-tuple-element.12.g, f32[8,128]{1,0:T(8,128)} %get-tuple-element.13.fac, bf16[768,768]{1,0:T(8,128)(2,1)} %w.1, f32[6,128]{1,0:T(8,128)} %get-tuple-element.14.ff_in, ...), custom_call_target="tpu_custom_call" | custom-call | tf_op jit(solution)/shard_map/write_results/pallas_call | solution.py:401
